TPU v7x, 32 devices: a whole 2x2x4 slice. The times are simulated.
32 devices in a mesh: row: 4 (over y, core), col: 8 (over z, x).
Axes of the slice: x: 2, y: 2, z: 4, core: 2. Of those that a mesh axis runs over, the one named last changes fastest.
Arguments:
- child_fronts: float32 [2, 8192, 8192], P(None, 'row', 'col'), as said below
- parent_front: float32 [12288, 12288], P('row', 'col'), as said below
- child_map: int32 [2, 7168], replicated, may hold values from 0 to 12287, as said below
Outputs:
- child_factor: float32 [2, 8192, 1024], P(None, 'row', 'col')
- parent_factor: float32 [12288, 256], P('row', 'col')
- parent_schur: float32 [12288, 12288], P('row', 'col')
Inputs may be any that keep to these rules, and one draw needn't show every extreme that they name: child_fronts[k] and parent_front are symmetric positive definite. parent_front is symmetric positive definite. The entries of child_map[k] are distinct. Each aligned block of 1024 entries of child_map[k] names exactly 128 indices in each aligned block of 1536 parent indices.
All inputs are finite; a program needn't handle non-finite values.
Results may differ from a plain program's by a relative error of at most 0.0003.
Values sent between devices are 32-bit elements; how exact they have to be, the bound alone decides.
A program may use at most 256 MiB of HBM per device.

v0:
```python
from functools import partial

import jax
import jax.numpy as jnp
from jax import lax
from jax.sharding import PartitionSpec as P

PP = 256
NB = 256


exact_mode = lax.Precision.HIGHEST


def from_root(value, axis, source):
    kept = jnp.where(lax.axis_index(axis) == source, value, 0).astype(value.dtype)
    return lax.psum(kept, axis)


def outer_update(factor_rows, crossed):
    return jnp.einsum("kin,kjn->kij", factor_rows, crossed, precision=exact_mode)


def take_rows(block, order):
    return jax.vmap(lambda single, picks: jnp.take(single, picks, axis=0))(block, order)


def take_both(block, row_order, col_order):
    rows_first = take_rows(block, row_order)
    flipped = take_rows(jnp.swapaxes(rows_first, 1, 2), col_order)
    return jnp.swapaxes(flipped, 1, 2)


def eliminate(tiles, pivots, send_panel, send_corner, send_cross):
    members, tile_rows, tile_cols = tiles.shape
    row_index = lax.axis_index("row")
    col_index = lax.axis_index("col")
    global_rows = row_index * tile_rows + jnp.arange(tile_rows, dtype=jnp.int32)
    total_steps = pivots // NB
    identity = jnp.broadcast_to(jnp.eye(NB, dtype=jnp.float32), (members, NB, NB))
    collected = []
    current = send_panel(lax.slice_in_dim(tiles, 0, NB, axis=2), 0)
    for panel_step in range(total_steps):
        offset = panel_step * NB
        owner_row = offset // tile_rows
        within_row = offset - owner_row * tile_rows
        corner = send_corner(
            lax.slice_in_dim(current, within_row, within_row + NB, axis=1), owner_row
        )
        factor = jnp.linalg.cholesky(corner)
        inverse = jax.vmap(partial(jax.scipy.linalg.solve_triangular, lower=True))(factor, identity)
        solved = jnp.einsum("krn,kmn->krm", current, inverse, precision=exact_mode)
        factor_rows = jnp.where((global_rows >= offset)[None, :, None], solved, jnp.float32(0.0))
        cross_first = col_index * tile_cols
        cross_owner = cross_first // tile_rows
        local_first = jnp.clip(cross_first - row_index * tile_rows, 0, tile_rows - tile_cols)
        crossed = send_cross(
            lax.dynamic_slice_in_dim(factor_rows, local_first, tile_cols, axis=1), cross_owner
        )
        collected.append(factor_rows)
        if panel_step + 1 < total_steps:
            upcoming = offset + NB
            next_owner = upcoming // tile_cols
            next_within = upcoming - next_owner * tile_cols
            strip = lax.slice_in_dim(tiles, next_within, next_within + NB, axis=2) - outer_update(
                factor_rows, lax.slice_in_dim(crossed, next_within, next_within + NB, axis=1)
            )
            current = send_panel(strip, next_owner)
            left_part = lax.slice_in_dim(tiles, 0, next_within, axis=2) - outer_update(
                factor_rows, lax.slice_in_dim(crossed, 0, next_within, axis=1)
            )
            right_part = lax.slice_in_dim(
                tiles, next_within + NB, tile_cols, axis=2
            ) - outer_update(
                factor_rows, lax.slice_in_dim(crossed, next_within + NB, tile_cols, axis=1)
            )
            tiles = jnp.concatenate([left_part, strip, right_part], axis=2)
        else:
            tiles = tiles - outer_update(factor_rows, crossed)
    return (tiles, jnp.concatenate(collected, axis=2))


def inverse_list(targets, length, filler):
    sources = jnp.arange(targets.shape[0], dtype=jnp.int32)
    start = jnp.full((length,), filler, jnp.int32)
    return start.at[targets].set(sources, mode="drop")


def extend_add(tiles, child_map, parent_front):
    members, tile_rows, tile_cols = tiles.shape
    row_count = lax.axis_size("row")
    col_count = lax.axis_size("col")
    row_index = lax.axis_index("row")
    col_index = lax.axis_index("col")
    width = tile_rows * row_count
    pivots = width - child_map.shape[1]
    parent_rows = parent_front.shape[0]
    parent_cols = parent_front.shape[1]
    row_slots = tile_rows // row_count
    col_slots = tile_cols // col_count
    full_map = jnp.concatenate([jnp.zeros((members, pivots), jnp.int32), child_map], axis=1)
    positions = jnp.arange(width, dtype=jnp.int32)[None, :]
    row_keys = jnp.where(positions < pivots, row_count, full_map // parent_rows)
    col_keys = jnp.where(positions < pivots, col_count, full_map // parent_cols)
    row_orders = jnp.argsort(row_keys.reshape(members, row_count, tile_rows), axis=2, stable=True)
    col_orders = jnp.argsort(col_keys.reshape(members, col_count, tile_cols), axis=2, stable=True)
    row_blocks = jnp.arange(row_count, dtype=jnp.int32)
    col_blocks = jnp.arange(col_count, dtype=jnp.int32)
    row_live = jnp.clip((row_blocks + 1) * tile_rows - pivots, 0, tile_rows) // row_count
    col_live = jnp.clip((col_blocks + 1) * tile_cols - pivots, 0, tile_cols) // col_count
    row_seats = jnp.arange(row_slots, dtype=jnp.int32)
    col_seats = jnp.arange(col_slots, dtype=jnp.int32)
    own_row_live = row_live[row_index]
    send_row_pos = jnp.minimum(
        row_blocks[:, None] * own_row_live + row_seats[None, :], tile_rows - 1
    )
    send_row_keep = jnp.broadcast_to(
        row_seats[None, :] < own_row_live, (row_count, row_slots)
    ).reshape(-1)
    own_row_order = jnp.take(row_orders, row_index, axis=1)
    send_rows = jnp.take(own_row_order, send_row_pos.reshape(-1), axis=1)
    own_col_live = col_live[col_index]
    send_col_pos = jnp.minimum(
        col_blocks[:, None] * own_col_live + col_seats[None, :], tile_cols - 1
    )
    send_col_keep = jnp.broadcast_to(
        col_seats[None, :] < own_col_live, (col_count, col_slots)
    ).reshape(-1)
    own_col_order = jnp.take(col_orders, col_index, axis=1)
    send_cols = jnp.take(own_col_order, send_col_pos.reshape(-1), axis=1)
    picked = take_both(tiles, send_rows, send_cols)
    picked = jnp.where(
        send_row_keep[None, :, None] & send_col_keep[None, None, :], picked, jnp.float32(0.0)
    )
    outgoing = jnp.transpose(
        picked.reshape(members, row_count, row_slots, col_count, col_slots), (1, 3, 0, 2, 4)
    )
    flat = outgoing.reshape(row_count * col_count, members, row_slots, col_slots)
    arrived = lax.all_to_all(flat, ("row", "col"), split_axis=0, concat_axis=0, tiled=True)
    arrived = arrived.reshape(row_count, col_count, members, row_slots, col_slots)
    received = jnp.transpose(arrived, (2, 0, 3, 1, 4)).reshape(members, tile_rows, tile_cols)
    recv_row_pos = jnp.minimum(row_index * row_live[:, None] + row_seats[None, :], tile_rows - 1)
    recv_row_keep = (row_seats[None, :] < row_live[:, None]).reshape(-1)
    local_rows = jnp.take_along_axis(row_orders, recv_row_pos[None, :, :], axis=2)
    global_rows = (row_blocks[None, :, None] * tile_rows + local_rows).reshape(members, -1)
    target_rows = jnp.take_along_axis(full_map, global_rows, axis=1) - row_index * parent_rows
    target_rows = jnp.where(recv_row_keep[None, :], target_rows, parent_rows)
    recv_col_pos = jnp.minimum(col_index * col_live[:, None] + col_seats[None, :], tile_cols - 1)
    recv_col_keep = (col_seats[None, :] < col_live[:, None]).reshape(-1)
    local_cols = jnp.take_along_axis(col_orders, recv_col_pos[None, :, :], axis=2)
    global_cols = (col_blocks[None, :, None] * tile_cols + local_cols).reshape(members, -1)
    target_cols = jnp.take_along_axis(full_map, global_cols, axis=1) - col_index * parent_cols
    target_cols = jnp.where(recv_col_keep[None, :], target_cols, parent_cols)
    row_sources = jax.vmap(lambda targets: inverse_list(targets, parent_rows, tile_rows))(
        target_rows
    )
    col_sources = jax.vmap(lambda targets: inverse_list(targets, parent_cols, tile_cols))(
        target_cols
    )
    padded = jnp.concatenate([received, jnp.zeros((members, 1, tile_cols), jnp.float32)], axis=1)
    placed_rows = take_rows(padded, row_sources)
    flipped = jnp.swapaxes(placed_rows, 1, 2)
    flipped = jnp.concatenate([flipped, jnp.zeros((members, 1, parent_rows), jnp.float32)], axis=1)
    placed = jnp.swapaxes(take_rows(flipped, col_sources), 1, 2)
    merged = parent_front
    for which_child in range(members):
        merged = merged + placed[which_child]
    return merged


def child_panel(piece, owner):
    return from_root(piece, "col", owner)


def child_corner(piece, owner):
    return from_root(piece, "row", owner)


def child_cross(piece, owner):
    return from_root(piece, "row", owner)


def parent_panel(piece, owner):
    return from_root(piece, "col", owner)


def parent_corner(piece, owner):
    return from_root(piece, "row", owner)


def parent_cross(piece, owner):
    return from_root(piece, "row", owner)


def local(child_fronts, parent_front, child_map):
    col_count = lax.axis_size("col")
    row_index = lax.axis_index("row")
    col_index = lax.axis_index("col")
    tile_rows = child_fronts.shape[1]
    width = tile_rows * lax.axis_size("row")
    pivots = width - child_map.shape[1]
    updated, child_panels = eliminate(child_fronts, pivots, child_panel, child_corner, child_cross)
    merged = extend_add(updated, child_map, parent_front)
    parent_updated, parent_panels = eliminate(
        merged[None], PP, parent_panel, parent_corner, parent_cross
    )
    child_share = pivots // col_count
    child_factor = lax.dynamic_slice_in_dim(
        child_panels, col_index * child_share, child_share, axis=2
    )
    parent_share = PP // col_count
    parent_factor = lax.dynamic_slice_in_dim(
        parent_panels[0], col_index * parent_share, parent_share, axis=1
    )
    parent_rows = parent_front.shape[0]
    parent_cols = parent_front.shape[1]
    global_rows = row_index * parent_rows + jnp.arange(parent_rows, dtype=jnp.int32)
    global_cols = col_index * parent_cols + jnp.arange(parent_cols, dtype=jnp.int32)
    keep = (global_rows[:, None] >= PP) & (global_cols[None, :] >= PP)
    parent_schur = jnp.where(keep, parent_updated[0], jnp.float32(0.0))
    return (child_factor, parent_factor, parent_schur)


def solution(mesh):
    placed = (P(None, "row", "col"), P("row", "col"), P())
    return jax.shard_map(
        local,
        mesh=mesh,
        in_specs=placed,
        out_specs=(P(None, "row", "col"), P("row", "col"), P("row", "col")),
        check_vma=False,
    )
```

profile of v0, /device:TPU:0, one launch (start us, length us, event | category | flops | bytes accessed | tf_op | source)
XLA Modules:
  0.0 2980.6 jit_solution(7669326672541635233)
XLA Ops:
  25.7 156.8 %all-reduce.21.cloned.1.call-done = f32[2,2048,256]{1,2,0:T(8,128)} async-done(((f32[2,2048,256]{1,2,0:T(8,128)}), f32[2,2048,256]{1,2,0:T(8,128)}) %all-reduce.21.cloned.1.call-update) | async-done | bytes 4194320 | tf_op jit(solution)/shard_map/psum | solution.py:17
  184.5 33.2 %all-reduce.23.cloned.1.call-done = f32[2,256,256]{1,2,0:T(8,128)} async-done(((f32[2,256,256]{1,2,0:T(8,128)}), f32[2,256,256]{1,2,0:T(8,128)}) %all-reduce.23.cloned.1.call-update) | async-done | bytes 524304 | tf_op jit(solution)/shard_map/psum | solution.py:17
  220.0 23.5 custom-call.62
  243.6 19.7 custom-call.63
  263.9 23.5 custom-call.64
  291.8 39.5 %custom-call.65 = f32[2,2,128,128]{2,3,1,0:T(8,128)S(1)} custom-call(f32[2,2,128,128]{3,2,1,0:T(8,128)S(1)} %bitcast.415), custom_call_target="InvertDiagBlocksLowerTriangular" | custom-call | tf_op jit(solution)/shard_map/vmap(jit(_solve_triangular))/triangular_solve | solution.py:51
  347.6 46.1 %all-reduce.25.cloned.1.call-done = f32[2,1024,256]{1,2,0:T(8,128)} async-done(((f32[2,1024,256]{1,2,0:T(8,128)}), f32[2,1024,256]{1,2,0:T(8,128)}) %all-reduce.25.cloned.1.call-update) | async-done | bytes 2097168 | tf_op jit(solution)/shard_map/psum | solution.py:17
  405.0 156.5 %all-reduce.27.cloned.1.call-done = f32[2,2048,256]{1,2,0:T(8,128)} async-done(((f32[2,2048,256]{1,2,0:T(8,128)}), f32[2,2048,256]{1,2,0:T(8,128)}) %all-reduce.27.cloned.1.call-update) | async-done | bytes 4194320 | tf_op jit(solution)/shard_map/psum | solution.py:17
  563.4 33.1 %all-reduce.29.cloned.1.call-done = f32[2,256,256]{1,2,0:T(8,128)} async-done(((f32[2,256,256]{1,2,0:T(8,128)}), f32[2,256,256]{1,2,0:T(8,128)}) %all-reduce.29.cloned.1.call-update) | async-done | bytes 524304 | tf_op jit(solution)/shard_map/psum | solution.py:17
  599.0 23.9 custom-call.66
  622.9 19.7 custom-call.67
  643.2 23.5 custom-call.68
  671.2 39.5 %custom-call.69 = f32[2,2,128,128]{2,3,1,0:T(8,128)S(1)} custom-call(f32[2,2,128,128]{3,2,1,0:T(8,128)S(1)} %bitcast.416), custom_call_target="InvertDiagBlocksLowerTriangular" | custom-call | tf_op jit(solution)/shard_map/vmap(jit(_solve_triangular))/triangular_solve | solution.py:51
  738.4 13.6 convolution_subtract_fusion
  752.1 21.0 all-reduce.31.cloned.1.call-done
  784.2 156.5 %all-reduce.33.cloned.1.call-done = f32[2,2048,256]{1,2,0:T(8,128)} async-done(((f32[2,2048,256]{1,2,0:T(8,128)}), f32[2,2048,256]{1,2,0:T(8,128)}) %all-reduce.33.cloned.1.call-update) | async-done | bytes 4194320 | tf_op jit(solution)/shard_map/psum | solution.py:17
  942.6 33.2 %all-reduce.35.cloned.1.call-done = f32[2,256,256]{1,2,0:T(8,128)} async-done(((f32[2,256,256]{1,2,0:T(8,128)}), f32[2,256,256]{1,2,0:T(8,128)}) %all-reduce.35.cloned.1.call-update) | async-done | bytes 524304 | tf_op jit(solution)/shard_map/psum | solution.py:17
  978.2 23.7 custom-call.70
  1002.0 19.7 custom-call.71
  1024.2 23.5 custom-call.72
  1052.1 39.8 %custom-call.73 = f32[2,2,128,128]{2,3,1,0:T(8,128)S(1)} custom-call(f32[2,2,128,128]{3,2,1,0:T(8,128)S(1)} %bitcast.417), custom_call_target="InvertDiagBlocksLowerTriangular" | custom-call | tf_op jit(solution)/shard_map/vmap(jit(_solve_triangular))/triangular_solve | solution.py:51
  1122.0 33.9 %all-reduce.37.cloned.1.call-done = f32[2,1024,256]{1,2,0:T(8,128)} async-done(((f32[2,1024,256]{1,2,0:T(8,128)}), f32[2,1024,256]{1,2,0:T(8,128)}) %all-reduce.37.cloned.1.call-update) | async-done | bytes 2097168 | tf_op jit(solution)/shard_map/psum | solution.py:17
  1155.9 12.6 broadcast_select_fusion
  1192.4 11.5 gather_fusion.2
  1212.1 112.9 %all-reduce.39.cloned.1.call-done = f32[2,2048,256]{1,2,0:T(8,128)} async-done(((f32[2,2048,256]{1,2,0:T(8,128)}), f32[2,2048,256]{1,2,0:T(8,128)}) %all-reduce.39.cloned.1.call-update) | async-done | bytes 4194320 | tf_op jit(solution)/shard_map/psum | solution.py:17
  1336.4 23.8 all-reduce.41.cloned.1.call-done
  1362.6 23.5 custom-call.74
  1386.2 19.7 custom-call.75
  1406.5 23.9 custom-call.76
  1434.9 39.3 %custom-call.77 = f32[2,2,128,128]{2,3,1,0:T(8,128)S(1)} custom-call(f32[2,2,128,128]{3,2,1,0:T(8,128)S(1)} %bitcast.418), custom_call_target="InvertDiagBlocksLowerTriangular" | custom-call | tf_op jit(solution)/shard_map/vmap(jit(_solve_triangular))/triangular_solve | solution.py:51
  1485.1 12.5 maximum_subtract_fusion.2
  1497.6 14.8 maximum_subtract_fusion.1
  1512.4 24.2 all-reduce.43.cloned.1.call-done
  1536.5 22.6 maximum_subtract_fusion
  1559.2 18.0 copy.533
  1577.1 79.9 %gather_fusion.6 = f32[4096,1024]{1,0:T(8,128)} fusion(f32[2,2048,1024]{2,1,0:T(8,128)} %copy.533, s32[4096]{0:T(1024)S(1)} %bitcast.400), kind=kCustom, calls=%fused_computation.6 | custom fusion | bytes 33587200 | tf_op jit(solution)/shard_map/vmap(jit(_take))/gather | solution.py:25
  1657.1 17.3 copy.534
  1674.4 12.3 select_bitcast_fusion.2
  1686.7 51.7 %gather_fusion.7 = f32[2048,2048]{1,0:T(8,128)} fusion(f32[2,1024,2048]{2,1,0:T(8,128)} %select_bitcast_fusion.2, s32[2048]{0:T(1024)S(1)} %bitcast.403), kind=kCustom, calls=%fused_computation.7 | custom fusion | bytes 33570816 | tf_op jit(solution)/shard_map/vmap(jit(_take))/gather | solution.py:25
  1738.4 18.1 copy.535
  1779.8 18.6 copy.539
  1798.5 20.5 gather_fusion.4
  1819.5 34.9 %gather_fusion.5 = s32[4096]{0:T(1024)S(1)} fusion(s32[2,8192]{1,0:T(2,128)S(1)} %copy-done, s32[4096]{0:T(1024)S(1)} %bitcast.401), kind=kCustom, calls=%fused_computation.5 | custom fusion | bytes 65536 | tf_op jit(solution)/shard_map/jit(take_along_axis)/gather | solution.py:146
  1856.1 15.6 scatter_custom_fusion.1
  1871.8 17.7 gather_fusion.3
  1899.4 249.4 %all-to-all-done = f32[32,2,512,128]{3,2,1,0:T(8,128)} async-done(((f32[32,2,512,128]{3,2,1,0:T(8,128)}), f32[32,2,512,128]{3,2,1,0:T(8,128)}, u32[]{:S(2)}, u32[]{:S(2)}) %all-to-all-start) | async-done | bytes 16777248 | tf_op jit(solution)/shard_map/all_to_all | solution.py:139
  2148.8 17.8 copy.537
  2166.6 20.8 reshape.1091
  2187.4 12.2 concatenate.31
  2199.6 187.4 %gather_fusion.8 = f32[6144,1024]{1,0:T(8,128)} fusion(f32[2,2049,1024]{2,0,1:T(2,128)} %concatenate.31, s32[6144]{0:T(1024)S(1)} %bitcast.399), kind=kCustom, calls=%fused_computation.8 | custom fusion | bytes 50380800 | tf_op jit(solution)/shard_map/vmap(jit(_take))/gather | solution.py:25
  2387.0 37.3 %copy.538 = f32[2,3072,1024]{1,0,2:T(2,128)} copy(f32[2,3072,1024]{2,1,0:T(8,128)} %bitcast.406) | data formatting | bytes 50331648 | tf_op jit(solution)/shard_map/vmap(jit(_take))/gather | solution.py:25
  2424.3 17.9 select_bitcast_fusion.1
  2442.2 17.7 concatenate.32
  2459.8 124.7 %gather_fusion.9 = f32[3072,3072]{1,0:T(8,128)} fusion(f32[2,1025,3072]{2,0,1:T(2,128)} %concatenate.32, s32[3072]{0:T(1024)S(1)} %reshape.1295), kind=kCustom, calls=%fused_computation.9 | custom fusion | bytes 75522048 | tf_op jit(solution)/shard_map/vmap(jit(_take))/gather | solution.py:25
  2584.5 27.2 select_bitcast_fusion
  2611.7 18.4 fusion.113
  2632.1 139.9 %all-reduce.45.cloned.1.call-done = f32[1,3072,256]{1,2,0:T(8,128)} async-done(((f32[1,3072,256]{1,2,0:T(8,128)}), f32[1,3072,256]{1,2,0:T(8,128)}) %all-reduce.45.cloned.1.call-update) | async-done | bytes 3145744 | tf_op jit(solution)/shard_map/psum | solution.py:17
  2774.0 31.8 %all-reduce.47.cloned.1.call-done = f32[1,256,256]{1,2,0:T(8,128)} async-done(((f32[1,256,256]{1,2,0:T(8,128)}), f32[1,256,256]{1,2,0:T(8,128)}) %all-reduce.47.cloned.1.call-update) | async-done | bytes 262160 | tf_op jit(solution)/shard_map/psum | solution.py:17
  2807.9 11.7 custom-call.30
  2830.2 11.7 custom-call.32
  2849.1 19.7 custom-call.33
  2884.2 35.0 %all-reduce.49.cloned.1.call-done = f32[1536,256]{0,1:T(8,128)} async-done(((f32[1536,256]{0,1:T(8,128)}), f32[1536,256]{0,1:T(8,128)}) %all-reduce.49.cloned.1.call-update) | async-done | bytes 1572880 | tf_op jit(solution)/shard_map/psum | solution.py:17
  2919.2 35.2 %subtract_select_fusion = f32[3072,1536]{0,1:T(8,128)} fusion(f32[3072,256]{0,1:T(8,128)S(1)} %convolution_select_fusion, f32[1536,256]{0,1:T(8,128)} %all-reduce.49.cloned.1.call-done, pred[3072]{0:T(1024)(128)(4,1)S(1)} %fusion.80, pred[1536]{0:T(1024)(128)(4,1)S(1)} %add_compare_fusion, f32[2,3072,1536]{1,2,0:T(8,128)} %select_bitcast_fusion, ...), kind=kOutput, calls=%fused_computation.29 | convolution fusion | flops 14519107584 | bytes 80220672 | tf_op jit(solution)/shard_map/kin,kjn->kij/dot_general | solution.py:21
  2954.4 18.6 copy.547
  (381 shorter events, 298.3 us)
Async XLA Ops:
  8.0 174.5 %all-reduce.21.cloned.1.call-start = ((), (), s32[]{:S(2)}) async-start(), calls=%async_computation.1 | async-start | bytes 8388608 | tf_op jit(solution)/shard_map/psum | solution.py:17
  25.5 192.1 %all-reduce.23.cloned.1.call-start = ((), (), s32[]{:S(2)}) async-start(), calls=%async_computation.2 | async-start | bytes 1048576 | tf_op jit(solution)/shard_map/psum | solution.py:17
  184.4 209.3 %all-reduce.25.cloned.1.call-start = ((), (), s32[]{:S(2)}) async-start(), calls=%async_computation.3 | async-start | bytes 4194304 | tf_op jit(solution)/shard_map/psum | solution.py:17
  338.3 2.0 copy-start.1
  342.2 219.3 %all-reduce.27.cloned.1.call-start = ((), (), s32[]{:S(2)}) async-start(), calls=%async_computation.4 | async-start | bytes 8388608 | tf_op jit(solution)/shard_map/psum | solution.py:17
  405.0 191.6 %all-reduce.29.cloned.1.call-start = ((), (), s32[]{:S(2)}) async-start(), calls=%async_computation.5 | async-start | bytes 1048576 | tf_op jit(solution)/shard_map/psum | solution.py:17
  563.4 209.7 %all-reduce.31.cloned.1.call-start = ((), (), s32[]{:S(2)}) async-start(), calls=%async_computation.6 | async-start | bytes 4194304 | tf_op jit(solution)/shard_map/psum | solution.py:17
  717.6 2.0 copy-start.2
  721.5 219.1 %all-reduce.33.cloned.1.call-start = ((), (), s32[]{:S(2)}) async-start(), calls=%async_computation.7 | async-start | bytes 8388608 | tf_op jit(solution)/shard_map/psum | solution.py:17
  729.4 9.1 copy-start.8
  784.1 191.7 %all-reduce.35.cloned.1.call-start = ((), (), s32[]{:S(2)}) async-start(), calls=%async_computation.8 | async-start | bytes 1048576 | tf_op jit(solution)/shard_map/psum | solution.py:17
  942.6 213.3 %all-reduce.37.cloned.1.call-start = ((), (), s32[]{:S(2)}) async-start(), calls=%async_computation.9 | async-start | bytes 4194304 | tf_op jit(solution)/shard_map/psum | solution.py:17
  978.2 23.7 copy-start.10
  1052.1 48.3 %copy-start.32 = (s32[2,2]{1,0:T(2,128)}, s32[2,2]{1,0:T(2,128)S(1)}, u32[]{:S(2)}) copy-start(s32[2,2]{1,0:T(2,128)S(1)} %get-tuple-element.532) | copy-start | bytes 52
  1091.9 0.7 copy-start.11
  1100.4 2.0 copy-start.3
  1102.4 2.0 copy-start.14
  1104.3 68.4 %sort.39.cloned.1.call-start = ((), (), s32[]{:S(2)}) async-start(), calls=%async_computation.17 | async-start | bytes 393248 | tf_op jit(solution)/shard_map/jit(argsort)/sort | solution.py:105
  1106.6 82.4 %sort.37.cloned.1.call-start = ((), (), s32[]{:S(2)}) async-start(), calls=%async_computation.16 | async-start | bytes 393248 | tf_op jit(solution)/shard_map/jit(argsort)/sort | solution.py:106
  1107.9 217.1 %all-reduce.39.cloned.1.call-start = ((), (), s32[]{:S(2)}) async-start(), calls=%async_computation.10 | async-start | bytes 8388608 | tf_op jit(solution)/shard_map/psum | solution.py:17
  1108.2 3.4 copy-start.28
  1108.2 5.5 copy-start.24
  1108.2 2.7 copy-start.35
  1168.5 191.8 %all-reduce.41.cloned.1.call-start = ((), (), s32[]{:S(2)}) async-start(), calls=%async_computation.11 | async-start | bytes 1048576 | tf_op jit(solution)/shard_map/psum | solution.py:17
  1170.7 18.2 copy-start.19
  1204.1 132.3 %copy-start.12 = (s32[2,1024,1]{1,0,2:T(2,128)}, s32[2,1024,1]{1,0,2:T(2,128)S(1)}, u32[]{:S(2)}) copy-start(s32[2,1024,1]{1,0,2:T(2,128)S(1)} %gather.66) | copy-start | bytes 24580
  1326.9 209.7 %all-reduce.43.cloned.1.call-start = ((), (), s32[]{:S(2)}) async-start(), calls=%async_computation.12 | async-start | bytes 4194304 | tf_op jit(solution)/shard_map/psum | solution.py:17
  1336.4 94.4 %copy-start.33 = (s32[2,2]{1,0:T(2,128)S(1)}, s32[2,2]{1,0:T(2,128)}, u32[]{:S(2)}) copy-start(s32[2,2]{1,0:T(2,128)} %copy-done.32) | copy-start | bytes 52
  1361.5 114.0 %copy-start.22 = (pred[2048]{0:T(1024)(128)(4,1)S(1)}, pred[2048]{0:T(1024)(128)(4,1)}, u32[]{:S(2)}) copy-start(pred[2048]{0:T(1024)(128)(4,1)} %fusion.93) | copy-start | bytes 6148
  1481.1 1.9 copy-start.5
  1483.1 2.0 copy-start.9
  1485.0 12.5 copy-start.4
  1485.0 12.5 copy-start.6
  1657.1 17.3 copy-start.16
  1738.3 18.1 copy-start.7
  1738.3 18.1 copy-start.21
  1774.7 4.8 copy-start.25
  1774.7 5.0 copy-start.29
  1774.7 374.1 %all-to-all-start = ((f32[32,2,512,128]{3,2,1,0:T(8,128)}), f32[32,2,512,128]{3,2,1,0:T(8,128)}, u32[]{:S(2)}, u32[]{:S(2)}) async-start(f32[32,2,512,128]{3,2,1,0:T(8,128)} %bitcast.409), calls=%async_computation | async-start | bytes 33554432 | tf_op jit(solution)/shard_map/all_to_all | solution.py:139
  1779.4 992.6 %all-reduce.45.cloned.1.call-start = ((), (), s32[]{:S(2)}) async-start(), calls=%async_computation.13 | async-start | bytes 6291456 | tf_op jit(solution)/shard_map/psum | solution.py:17
  1779.8 18.7 copy-start.36
  1779.8 39.6 %copy-start.20 = (pred[2048]{0:T(1024)(128)(4,1)S(1)}, pred[2048]{0:T(1024)(128)(4,1)}, u32[]{:S(2)}) copy-start(pred[2048]{0:T(1024)(128)(4,1)} %get-tuple-element.208) | copy-start | bytes 6148
  1798.4 21.1 copy-start
  1819.5 35.0 %copy-start.31 = (s32[2]{0:T(128)S(1)}, s32[2]{0:T(128)}, u32[]{:S(2)}) copy-start(s32[2]{0:T(128)} %constant.441) | copy-start | bytes 28
  1819.5 35.6 %copy-start.26 = (s32[2]{0:T(128)S(1)}, s32[2]{0:T(128)}, u32[]{:S(2)}) copy-start(s32[2]{0:T(128)} %constant.438) | copy-start | bytes 28
  1854.4 17.3 copy-start.17
  1871.7 17.8 copy-start.13
  1871.8 17.8 copy-start.15
  1871.8 17.8 copy-start.23
  1871.8 17.8 copy-start.30
  1871.8 18.2 copy-start.27
  2459.8 124.7 %copy-start.18 = (pred[2,1536]{1,0:T(4,128)(4,1)S(1)}, pred[2,1536]{1,0:T(4,128)(4,1)}, u32[]{:S(2)}) copy-start(pred[2,1536]{1,0:T(4,128)(4,1)} %compare_and_fusion.2) | copy-start | bytes 9220
  2632.1 212.6 %copy-start.34 = (s32[2,2]{1,0:T(2,128)S(1)}, s32[2,2]{1,0:T(2,128)}, u32[]{:S(2)}) copy-start(s32[2,2]{1,0:T(2,128)} %copy-done.32) | copy-start | bytes 52
  2632.1 173.7 %all-reduce.47.cloned.1.call-start = ((), (), s32[]{:S(2)}) async-start(), calls=%async_computation.14 | async-start | bytes 524288 | tf_op jit(solution)/shard_map/psum | solution.py:17
  2773.7 145.5 %all-reduce.49.cloned.1.call-start = ((), (), s32[]{:S(2)}) async-start(), calls=%async_computation.15 | async-start | bytes 3145728 | tf_op jit(solution)/shard_map/psum | solution.py:17
Sparse Core Ops, SparseCore 0:
  25.7 156.7 all-reduce.20
  185.4 32.2 all-reduce.22
  342.3 51.3 all-reduce.24
  405.1 156.3 all-reduce.26
  564.4 32.1 all-reduce.28
  721.7 51.3 all-reduce.30
  784.3 156.3 all-reduce.32
  943.6 32.2 all-reduce.34
  1104.5 51.3 all-reduce.36
  1168.6 156.3 all-reduce.38
  1328.0 32.1 all-reduce.40
  1485.1 51.3 all-reduce.42
  2632.2 139.7 all-reduce.44
  2774.9 30.9 all-reduce.46
  2876.3 42.8 all-reduce.48
Sparse Core Ops, SparseCore 1:
  1107.3 6.2 sort.43.cloned.1.call-done
  1116.1 6.9 sort.41.cloned.1.call-done
  (2 shorter events, 0.0 us)
where the time goes:
time: 3000 us; the launch traced here: 2980 us
  waiting for transfers between devices  1290 us (43%)
  local copies, waits for them, and re-layouts  861 us (29%)
  other arithmetic  617 us (21%)
  matrix products  190 us (6%)
    psum x15, waiting for transfers between devices, from_root(): return lax.psum(kept, axis)  1040 us
    gather x8, local copies, waits for them, and re-layouts, take_rows(): jnp.take(single, picks, axis=0)  516 us
    another operation x40, other arithmetic, eliminate(): factor = jnp.linalg.cholesky(corner)  303 us
    all_to_all x1, waiting for transfers between devices, extend_add(): lax.all_to_all(flat, ('row', 'col'), split_axis=0, concat_axis=0, tiled=T...  249 us
    another operation x12, other arithmetic, eliminate(): jax.vmap(partial(jax.scipy.linalg.solve_triangular, lower=True))  178 us
    dot_general x10, matrix products, outer_update(): jnp.einsum('kin,kjn->kij', factor_rows, crossed, precision=exact_mode)  151 us
    unnamed x114, local copies, waits for them, and re-layouts  99 us
  transfers between devices with their start and end apart: 16, of which 16 were waited for; matrix products, arithmetic and copies ran while one was open for 9% of the time, Pallas kernels for 0%

commit v1 on v0

v1 whole, which is shorter than its diff:
```python
from functools import partial

import jax
import jax.numpy as jnp
from jax import lax
from jax.experimental import pallas as pl
from jax.experimental.pallas import tpu as pltpu
from jax.sharding import PartitionSpec as P

PP = 256
SUB = 128
FULL = lax.Precision.HIGHEST
THREE = lax.Precision.HIGH
CONTRACT_LAST = (((1,), (1,)), ((), ()))


def mul_t(a, b, precision=FULL):
    return lax.dot_general(
        a, b, CONTRACT_LAST, precision=precision, preferred_element_type=jnp.float32
    )


def inverse_factors(blocks):
    lane = lax.broadcasted_iota(jnp.int32, (8, SUB), 1)
    sub = lax.broadcasted_iota(jnp.int32, (8, SUB), 0)
    groups = SUB // 8
    work = [[block[8 * g : 8 * g + 8, :] for g in range(groups)] for block in blocks]
    for k in range(SUB):
        first, r = divmod(k, 8)
        for m in work:
            row = m[first][r : r + 1, :]
            scaled = jnp.where(lane[0:1] == k, 1.0, row) / row[:, k : k + 1]
            scaled = jnp.broadcast_to(scaled, (8, SUB))
            for g in range(first, groups):
                if g == first and r == 7:
                    continue
                col = jnp.broadcast_to(m[g][:, k : k + 1], (8, SUB))
                if g == first:
                    below = sub > r
                    col = jnp.where(below, col, 0.0)
                    base = jnp.where((lane == k) & below, 0.0, m[g])
                else:
                    base = jnp.where(lane == k, 0.0, m[g])
                m[g] = base - col * scaled
    results = []
    for m in work:
        rows = []
        for g in range(groups):
            spot = sub + 8 * g
            diag = jnp.sum(jnp.where(lane == spot, m[g], 0.0), axis=1, keepdims=True)
            unit = jnp.where(lane < spot, m[g], jnp.where(lane == spot, 1.0, 0.0))
            rows.append(unit * lax.rsqrt(jnp.broadcast_to(diag, (8, SUB))))
        results.append(jnp.concatenate(rows, axis=0))
    return results


def factor_kernel(members, width, tall, chunk, a_ref, x_ref, out_ref, work_ref, panel_ref):
    steps = width // SUB
    work_ref[...] = a_ref[...]
    out_ref[...] = x_ref[...]

    def step(p, carry):
        at = pl.multiple_of(p * SUB, SUB)
        cols = pl.ds(at, SUB)
        inverses = inverse_factors([work_ref[k, cols, cols] for k in range(members)])
        for k in range(members):
            inverse = inverses[k]
            solved = mul_t(work_ref[k, :, cols], inverse)
            rows = lax.broadcasted_iota(jnp.int32, (width, SUB), 0)
            panel_ref[k] = jnp.where(rows >= at + SUB, solved, 0.0)

            def trailing(b, c):
                spot = pl.ds(pl.multiple_of(b * SUB, SUB), SUB)
                work_ref[k, spot, :] -= mul_t(panel_ref[k, spot, :], panel_ref[k])
                return c

            lax.fori_loop(p + 1, steps, trailing, 0)

            def own(b, c):
                spot = pl.ds(pl.multiple_of(b * chunk, chunk), chunk)
                ours = mul_t(out_ref[k, spot, cols], inverse)
                out_ref[k, spot, :] -= mul_t(ours, panel_ref[k])
                out_ref[k, spot, cols] = ours
                return c

            lax.fori_loop(0, tall // chunk, own, 0)
        return carry

    lax.fori_loop(0, steps, step, 0)


def factor_rows(corner, rows):
    members, width, _ = corner.shape
    tall = rows.shape[1]
    chunk = min(tall, 256)
    vmem = pl.BlockSpec(memory_space=pltpu.VMEM)
    return pl.pallas_call(
        partial(factor_kernel, members, width, tall, chunk),
        out_shape=jax.ShapeDtypeStruct(rows.shape, jnp.float32),
        in_specs=[vmem, vmem],
        out_specs=vmem,
        scratch_shapes=[
            pltpu.VMEM((members, width, width), jnp.float32),
            pltpu.VMEM((members, width, SUB), jnp.float32),
        ],
        compiler_params=pltpu.CompilerParams(vmem_limit_bytes=48 * 1024 * 1024),
    )(corner, rows)


def take_rows(block, picks):
    return jax.vmap(lambda one, at: jnp.take(one, at, axis=0, mode="clip"))(block, picks)


def local(child_fronts, parent_front, child_map):
    nr = lax.axis_size("row")
    nc = lax.axis_size("col")
    i = lax.axis_index("row")
    j = lax.axis_index("col")
    members, tr, tc = child_fronts.shape
    prow, pcol = parent_front.shape
    width = tr * nr
    pivots = width - child_map.shape[1]
    pb = pivots // tc
    nb = nc
    q = tc // nc
    js = nc // nr
    br = tr // tc

    with jax.named_scope("orders"):
        positions = jnp.arange(width, dtype=jnp.int32)
        full_map = jnp.concatenate(
            [jnp.zeros((members, pivots), jnp.int32), child_map], axis=1
        )
        keys = jnp.where(positions[None] < pivots, (positions % tc)[None] // q, full_map // pcol)
        order = jnp.argsort(keys.reshape(members, nb, tc), axis=2, stable=True)
        targets = jnp.take_along_axis(full_map.reshape(members, nb, tc), order, axis=2)
        targets = targets.reshape(members, nb, nc, q)

        def slots(tgt):
            flat = tgt[pb:].reshape(-1)
            fill = jnp.full((pcol,), nb * q, jnp.int32)
            return fill.at[flat].set(jnp.arange(flat.shape[0], dtype=jnp.int32) + pb * q)

        def slots_of(block):
            rel = jnp.take(targets, block, axis=2) - block * pcol
            return jax.vmap(slots)(rel)

        row_slots = [slots_of(i * js + s) for s in range(js)]
        col_slots = slots_of(j)

    with jax.named_scope("corner"):
        pieces = []
        for b in range(pb):
            mine = jnp.where((i == 0) & (j == b), child_fronts[:, :pivots, :], 0.0)
            pieces.append(lax.psum(mine, ("row", "col")))
        corner = jnp.concatenate(pieces, axis=2)

    with jax.named_scope("own_rows"):
        own_order = jnp.take(order, j, axis=1)
        strips = take_rows(jnp.swapaxes(child_fronts[:, :pivots, :], 1, 2), own_order)
        strips = strips.reshape(members, nr, tc // nr, pivots)
        own = jnp.where(i == 0, strips[:, 0], 0.0)
        for t in range(1, nr):
            own = own + lax.ppermute(strips[:, t], "row", [(0, t)])

    with jax.named_scope("exchange"):
        row_order = lax.dynamic_slice_in_dim(order, i * br, br, axis=1)
        row_order = row_order + (jnp.arange(br, dtype=jnp.int32) * tc)[None, :, None]
        row_order = row_order.reshape(members, br, nr, js * q)
        row_order = jnp.swapaxes(row_order, 1, 2).reshape(members, tr)
        picked = take_rows(child_fronts, row_order)
        picked = take_rows(jnp.swapaxes(picked, 1, 2), own_order)
        outgoing = picked.reshape(members, nc, q, nr, br * js * q)
        outgoing = jnp.transpose(outgoing, (3, 1, 0, 2, 4)).reshape(
            nr * nc, members, q, br * js * q
        )
        arrived = lax.all_to_all(outgoing, ("row", "col"), split_axis=0, concat_axis=0, tiled=True)
        arrived = arrived.reshape(nr, nc, members, q, br, js, q)
        arrived = jnp.transpose(arrived, (2, 1, 3, 5, 0, 4, 6)).reshape(
            members, nc * q, js * nb * q
        )

    with jax.named_scope("child_factor"):
        factor = factor_rows(corner, own)
        place = jnp.take(order, j, axis=1).reshape(members, nr, tc // nr)
        place = jnp.take(place, i, axis=1) + j * tc
        panel_start = (jnp.arange(pivots, dtype=jnp.int32) // 256) * 256
        factor = jnp.where(place[:, :, None] >= panel_start[None, None, :], factor, 0.0)

    with jax.named_scope("factor_rows"):
        gathered = lax.all_gather(factor, "col", axis=0, tiled=False)
        gathered = gathered.reshape(nc, members, js, q, pivots)
        owner = j // js
        cross = jnp.take(gathered, j % js, axis=2)
        cross = lax.psum(jnp.where(i == owner, cross, 0.0), "row")

        def placed(rows, slots):
            flat = jnp.swapaxes(rows, 0, 1).reshape(members, nb * q, pivots)
            got = take_rows(flat, slots)
            got = jnp.where((slots < nb * q)[:, :, None], got, 0.0)
            return jnp.concatenate([got[k] for k in range(members)], axis=1)

        left = jnp.concatenate(
            [placed(gathered[:, :, s], row_slots[s]) for s in range(js)], axis=0
        )
        right = placed(cross, col_slots)

    with jax.named_scope("place"):
        row_all = jnp.concatenate(
            [
                jnp.where(row_slots[s] < nb * q, row_slots[s] + s * nb * q, js * nb * q)
                for s in range(js)
            ],
            axis=1,
        )
        by_col = take_rows(arrived, col_slots)
        by_col = jnp.where((col_slots < nb * q)[:, :, None], by_col, 0.0)
        by_row = take_rows(jnp.swapaxes(by_col, 1, 2), row_all)
        by_row = jnp.where((row_all < js * nb * q)[:, :, None], by_row, 0.0)
        base = parent_front
        for k in range(members):
            base = base + by_row[k]

    with jax.named_scope("parent_strips"):
        row_strip = base[:PP, :] - mul_t(left[:PP], right, THREE)
        col_strip = base[:, :PP] - mul_t(left, right[:PP], THREE)
        row_strip = lax.psum(jnp.where(i == 0, row_strip, 0.0), "row")
        col_strip = lax.psum(jnp.where(j == 0, col_strip, 0.0), "col")
        head = lax.psum(jnp.where((i == 0) & (j == 0), col_strip[:PP], 0.0), ("row", "col"))

    with jax.named_scope("merged"):
        merged = base - mul_t(left, right, THREE)

    with jax.named_scope("parent_factor"):
        rows = jnp.concatenate([col_strip, row_strip.T], axis=0)
        solved = factor_rows(head[None], rows[None])[0]
        solved_rows = solved[:prow]
        solved_cols = solved[prow:]

    with jax.named_scope("parent_schur"):
        global_rows = i * prow + jnp.arange(prow, dtype=jnp.int32)
        global_cols = j * pcol + jnp.arange(pcol, dtype=jnp.int32)
        keep = (global_rows[:, None] >= PP) & (global_cols[None, :] >= PP)
        schur = jnp.where(keep, merged - mul_t(solved_rows, solved_cols, THREE), 0.0)

    with jax.named_scope("outputs"):
        share = PP // nc
        parent_factor = lax.dynamic_slice_in_dim(solved_rows, j * share, share, axis=1)
        cshare = pivots // nc
        pieces = factor.reshape(members, tc // nr, nc, cshare)
        pieces = lax.all_to_all(pieces, "col", split_axis=2, concat_axis=0, tiled=False)
        pieces = pieces.reshape(nr, br, members, tc // nr, cshare)
        pieces = lax.all_to_all(pieces, "row", split_axis=0, concat_axis=0, tiled=True)
        pieces = jnp.transpose(pieces, (2, 1, 0, 3, 4)).reshape(members, tr, cshare)
        natural = jnp.argsort(lax.dynamic_slice_in_dim(order, i * br, br, axis=1), axis=2)
        natural = natural + (jnp.arange(br, dtype=jnp.int32) * tc)[None, :, None]
        child_factor = take_rows(pieces, natural.reshape(members, tr))
    return (child_factor, parent_factor, schur)


def solution(mesh):
    return jax.shard_map(
        local,
        mesh=mesh,
        in_specs=(P(None, "row", "col"), P("row", "col"), P()),
        out_specs=(P(None, "row", "col"), P("row", "col"), P("row", "col")),
        check_vma=False,
    )
```

time: 3000 us -> 2360 us (0.79)
  waiting for transfers between devices: 1290 us -> 526 us
  other arithmetic: 617 us -> 154 us
  local copies, waits for them, and re-layouts: 861 us -> 1280 us
  Pallas kernels: 0 us -> 209 us
  matrix products: 190 us -> 119 us
    psum x15 -> x5, waiting for transfers between devices: 1040 us -> 260 us  [the longest x1 128 us: local(): lax.psum(jnp.where((i == 0) & (j == 0), col_strip[:PP], 0.0), ('row', 'co...]
    another operation x52 -> x0, other arithmetic: 482 us -> none  [the longest x40 303 us: eliminate(): factor = jnp.linalg.cholesky(corner)]
    gather x22, local copies, waits for them, and re-layouts: 615 us -> 1020 us  [the longest x20 894 us: take_rows(): jnp.take(one, at, axis=0, mode='clip')]
    pallas_call x0 -> x2, Pallas kernels: none -> 209 us  [factor_rows(): pl.pallas_call(partial(factor_kernel, members, width, tall, chunk), out_s...]
    dot_general x15 -> x4, matrix products: 179 us -> 119 us  [mul_t(): lax.dot_general(a, b, CONTRACT_LAST, precision=precision, preferred_eleme...]
    ppermute x0 -> x3, waiting for transfers between devices: none -> 47.8 us  [local(): own = own + lax.ppermute(strips[:, t], 'row', [(0, t)])]
    squeeze x0 -> x5, local copies, waits for them, and re-layouts: none -> 44.6 us  [the longest x3 35.7 us: placed(): return jnp.concatenate([got[k] for k in range(members)], axis=1)]
    reshape x2 -> x8, local copies, waits for them, and re-layouts: 21.5 us -> 59.8 us  [the longest x2 36.4 us: local(): outgoing = picked.reshape(members, nc, q, nr, br * js * q)]
  transfers between devices with their start and end apart: 16 -> 12, of which waited for: 16 -> 8; matrix products, arithmetic and copies ran while one was open for 9% -> 61% of each run, Pallas kernels for 0% -> 0%
where the time goes in v1:
time: 2360 us; the launch traced here: 2340 us
  local copies, waits for them, and re-layouts  1280 us (54%)
  waiting for transfers between devices  526 us (22%)
  Pallas kernels  209 us (9%)
  other arithmetic  154 us (7%)
  matrix products  119 us (5%)
  starting transfers between devices  30.5 us (1%)
    gather x20, local copies, waits for them, and re-layouts, take_rows(): jnp.take(one, at, axis=0, mode='clip')  894 us
    pallas_call x2, Pallas kernels, factor_rows(): pl.pallas_call(partial(factor_kernel, members, width, tall, chunk), out_s...  209 us
    all_to_all x1, waiting for transfers between devices, local(): lax.all_to_all(outgoing, ('row', 'col'), split_axis=0, concat_axis=0, til...  194 us
    psum x1, waiting for transfers between devices, local(): lax.psum(jnp.where((i == 0) & (j == 0), col_strip[:PP], 0.0), ('row', 'co...  128 us
    gather x2, local copies, waits for them, and re-layouts, local(): jnp.take_along_axis(full_map.reshape(members, nb, tc), order, axis=2)  126 us
    dot_general x4, matrix products, mul_t(): lax.dot_general(a, b, CONTRACT_LAST, precision=precision, preferred_eleme...  119 us
    unnamed x68, local copies, waits for them, and re-layouts  74.5 us
    psum x1, waiting for transfers between devices, local(): pieces.append(lax.psum(mine, ('row', 'col')))  64.7 us
  transfers between devices with their start and end apart: 12, of which 8 were waited for; matrix products, arithmetic and copies ran while one was open for 61% of the time, Pallas kernels for 0%

profile of v1, /device:TPU:0, one launch (start us, length us, event | category | flops | bytes accessed | tf_op | source)
XLA Modules:
  0.0 2335.7 jit_solution(8927553987371890294)
XLA Ops:
  11.0 12.5 slice_bitcast_fusion.2
  23.6 8.8 copy.71
  33.3 40.2 %gather_fusion = f32[2048,1024]{1,0:T(8,128)} fusion(f32[2,1024,1024]{2,1,0:T(8,128)} %copy.71, s32[2048]{0:T(1024)S(1)} %bitcast.195), kind=kCustom, calls=%fused_computation | custom fusion | bytes 16793600 | tf_op jit(solution)/shard_map/own_rows/vmap(jit(_take))/gather | solution.py:111
  73.4 5.8 slice_bitcast_fusion.11
  79.3 2.4 collective-permute-start
  81.7 4.6 collective-permute-start.1
  86.4 2.6 collective-permute-start.2
  89.1 22.5 collective-permute-done.1
  111.6 25.3 %collective-permute-done.2 = f32[2,256,1024]{2,1,0:T(8,128)} collective-permute-done((f32[2,256,1024]{2,1,0:T(8,128)}, f32[2,256,1024]{2,1,0:T(8,128)}, u32[]{:S(2)}, u32[]{:S(2)}) %collective-permute-start.2) | collective-permute-done | bytes 2097184 | tf_op jit(solution)/shard_map/own_rows/ppermute | solution.py:164
  136.9 4.5 fusion.21.x_ref
  141.4 64.7 %all-reduce.7.cloned.1.call-done.a_ref = f32[2,1024,1024]{2,1,0:T(8,128)} async-done(((f32[2,1024,1024]{2,1,0:T(8,128)}), f32[2,1024,1024]{2,1,0:T(8,128)}) %all-reduce.7.cloned.1.call-update) | async-done | bytes 8388624 | tf_op jit(solution)/shard_map/corner/psum | solution.py:155
  206.1 156.1 %child_factor.1 = f32[2,256,1024]{2,1,0:T(8,128)S(1)} custom-call(f32[2,1024,1024]{2,1,0:T(8,128)} %all-reduce.7.cloned.1.call-done.a_ref, f32[2,256,1024]{2,1,0:T(8,128)S(1)} %fusion.21.x_ref), custom_call_target="tpu_custom_call" | custom-call | tf_op jit(solution)/shard_map/child_factor/pallas_call | solution.py:97
  364.5 83.1 %gather_fusion.3 = f32[4096,1024]{1,0:T(8,128)} fusion(f32[2,2048,1024]{2,1,0:T(8,128)} %param.7, s32[4096]{0:T(1024)S(1)} %bitcast.198), kind=kCustom, calls=%fused_computation.3 | custom fusion | bytes 33587200 | tf_op jit(solution)/shard_map/exchange/vmap(jit(_take))/gather | solution.py:111
  447.6 16.8 copy.79
  464.4 51.4 %gather_fusion.4 = f32[2048,2048]{1,0:T(8,128)} fusion(f32[2,1024,2048]{2,1,0:T(8,128)} %bitcast.193, s32[2048]{0:T(1024)S(1)} %bitcast.196), kind=kCustom, calls=%fused_computation.4 | custom fusion | bytes 33570816 | tf_op jit(solution)/shard_map/exchange/vmap(jit(_take))/gather | solution.py:111
  515.9 20.5 reshape.283
  536.3 16.0 copy.80
  552.3 5.8 all-to-all-start.2
  558.3 18.6 copy.85
  577.0 126.3 %gather_fusion.2 = s32[16384]{0:T(1024)S(1)} fusion(s32[2,8,1024]{2,1,0:T(8,128)S(1)} %bitcast.190, s32[16384]{0:T(1024)S(1)} %bitcast.194), kind=kCustom, calls=%fused_computation.2 | custom fusion | bytes 327680 | tf_op jit(solution)/shard_map/orders/jit(take_along_axis)/gather | solution.py:136
  703.6 18.1 constant_dynamic-slice_fusion.1
  721.6 8.7 fusion.5
  731.2 7.1 scatter_custom_fusion.2
  738.5 7.1 scatter_custom_fusion.1
  745.7 7.3 scatter_custom_fusion
  758.4 193.7 %all-to-all-done.2 = f32[32,2,128,512]{3,2,1,0:T(8,128)} async-done(((f32[32,2,128,512]{3,2,1,0:T(8,128)}), f32[32,2,128,512]{3,2,1,0:T(8,128)}, u32[]{:S(2)}, u32[]{:S(2)}) %all-to-all-start.2) | async-done | bytes 16777248 | tf_op jit(solution)/shard_map/exchange/all_to_all | solution.py:177
  952.2 11.1 all-to-all-start
  963.4 17.4 copy.81
  980.8 25.1 %copy.82 = f32[2,8,128,2,4,2,128]{6,5,4,3,2,1,0:T(2,128)} copy(f32[2,8,128,2,4,2,128]{2,6,3,5,0,1,4:T(8,128)} %bitcast.205) | data formatting | bytes 33554432 | tf_op jit(solution)/shard_map/exchange/transpose | solution.py:179
  1005.9 21.7 reshape.286
  1027.6 109.8 %gather_fusion.5 = f32[3072,2048]{1,0:T(8,128)} fusion(f32[2,1024,2048]{2,1,0:T(8,128)} %reshape.286, s32[3072]{0:T(1024)S(1)} %reshape.542), kind=kCustom, calls=%fused_computation.5 | custom fusion | bytes 50356224 | tf_op jit(solution)/shard_map/place/vmap(jit(_take))/gather | solution.py:111
  1137.4 24.7 %copy.83 = f32[2,1536,2048]{1,2,0:T(8,128)} copy(f32[2,1536,2048]{2,1,0:T(8,128)} %bitcast.202) | data formatting | bytes 50331648 | tf_op jit(solution)/shard_map/place/vmap(jit(_take))/gather | solution.py:111
  1162.1 17.3 select_bitcast_fusion
  1179.4 203.4 %gather_fusion.6 = f32[6144,1536]{1,0:T(8,128)} fusion(f32[2,2048,1536]{2,1,0:T(8,128)} %select_bitcast_fusion, s32[6144]{0:T(1024)S(1)} %bitcast.197), kind=kCustom, calls=%fused_computation.6 | custom fusion | bytes 75546624 | tf_op jit(solution)/shard_map/place/vmap(jit(_take))/gather | solution.py:111
  1382.8 36.8 %copy.84 = f32[2,3072,1536]{1,2,0:T(8,128)} copy(f32[2,3072,1536]{2,1,0:T(8,128)} %bitcast.201) | data formatting | bytes 75497472 | tf_op jit(solution)/shard_map/place/vmap(jit(_take))/gather | solution.py:111
  1419.6 29.4 %broadcast_select_fusion = f32[2,3072,1536]{1,2,0:T(8,128)} fusion(f32[2,3072,1536]{1,2,0:T(8,128)} %copy.84, pred[2,3072]{1,0:T(4,128)(4,1)S(1)} %copy-done.15), kind=kLoop, calls=%fused_computation.20 | loop fusion | flops 9437184 | bytes 75503616 | tf_op jit(solution)/shard_map/place/jit(_where)/select_n | solution.py:219
  1449.0 25.9 %fusion = f32[3072,1536]{0,1:T(8,128)} fusion(f32[2,3072,1536]{1,2,0:T(8,128)} %broadcast_select_fusion, f32[3072,1536]{0,1:T(8,128)} %copy.85), kind=kLoop, calls=%fused_computation.16 | loop fusion | flops 9437184 | bytes 75497472 | tf_op jit(solution)/shard_map/place/add | solution.py:222
  1474.9 4.1 copy.107
  1479.0 93.5 %gather_fusion.7 = f32[3072,1024]{1,0:T(8,128)} fusion(f32[2,1024,1024]{2,1,0:T(8,128)} %bitcast.191, s32[3072]{0:T(1024)S(1)} %copy-done.4), kind=kCustom, calls=%fused_computation.7 | custom fusion | bytes 25190400 | tf_op jit(solution)/shard_map/factor_rows/vmap(jit(_take))/gather | solution.py:111
  1572.5 10.2 broadcast_select_fusion.3
  1582.8 12.0 slice_bitcast_fusion.8
  1594.7 8.3 copy.108
  1603.0 93.9 %gather_fusion.8 = f32[3072,1024]{1,0:T(8,128)} fusion(f32[2,1024,1024]{2,1,0:T(8,128)} %bitcast.192, s32[3072]{0:T(1024)S(1)} %copy-done.3), kind=kCustom, calls=%fused_computation.8 | custom fusion | bytes 25190400 | tf_op jit(solution)/shard_map/factor_rows/vmap(jit(_take))/gather | solution.py:111
  1696.9 10.2 broadcast_select_fusion.2
  1707.1 11.8 slice_bitcast_fusion.6
  1719.0 94.2 %gather_fusion.9 = f32[3072,1024]{1,0:T(8,128)} fusion(f32[2,1024,1024]{2,1,0:T(8,128)} %all-reduce.9.cloned.1.call-done, s32[3072]{0:T(1024)S(1)} %copy-done.2), kind=kCustom, calls=%fused_computation.9 | custom fusion | bytes 25190400 | tf_op jit(solution)/shard_map/factor_rows/vmap(jit(_take))/gather | solution.py:111
  1813.2 10.2 broadcast_select_fusion.1
  1823.4 11.9 slice_bitcast_fusion.4
  1835.2 22.3 fusion.7
  1857.6 3.1 copy.77
  1860.7 3.6 all-to-all-start.1
  1865.3 24.7 %all-to-all-done.1 = f32[4,2,2,256,128]{4,3,1,2,0:T(8,128)S(1)} async-done(((f32[4,2,2,256,128]{4,3,1,2,0:T(8,128)}), f32[4,2,2,256,128]{4,3,1,2,0:T(8,128)S(1)}, u32[]{:S(2)}, u32[]{:S(2)}) %all-to-all-start.1) | async-done | bytes 2097184 | tf_op jit(solution)/shard_map/outputs/all_to_all | solution.py:253
  1893.1 45.0 %gather_fusion.1 = f32[4096,128]{1,0:T(8,128)} fusion(f32[2,2048,128]{2,1,0:T(8,128)S(1)} %bitcast.200, s32[4096]{0:T(1024)S(1)} %bitcast.199), kind=kCustom, calls=%fused_computation.1 | custom fusion | bytes 4227072 | tf_op jit(solution)/shard_map/outputs/vmap(jit(_take))/gather | solution.py:111
  1938.1 9.8 fusion.12
  1948.0 12.4 pad_maximum_fusion.14
  1960.4 27.2 %all-reduce.11.cloned.1.call-done = f32[3072,256]{0,1:T(8,128)} async-done(((f32[3072,256]{0,1:T(8,128)}), f32[3072,256]{0,1:T(8,128)}) %all-reduce.11.cloned.1.call-update) | async-done | bytes 3145744 | tf_op jit(solution)/shard_map/parent_strips/psum | solution.py:228
  1991.7 40.1 %all-reduce.15.cloned.1.call-done = f32[1536,256]{1,0:T(8,128)} async-done(((f32[1536,256]{1,0:T(8,128)}), f32[1536,256]{1,0:T(8,128)}) %all-reduce.15.cloned.1.call-update) | async-done | bytes 1572880 | tf_op jit(solution)/shard_map/parent_strips/psum | solution.py:227
  2031.8 3.9 maximum_bitcast_fusion.x_ref
  2035.6 128.0 %all-reduce.13.cloned.1.call-done = f32[1,256,256]{1,2,0:T(8,128)} async-done(((f32[1,256,256]{1,2,0:T(8,128)}), f32[1,256,256]{1,2,0:T(8,128)}) %all-reduce.13.cloned.1.call-update) | async-done | bytes 262160 | tf_op jit(solution)/shard_map/parent_strips/psum | solution.py:229
  2164.8 53.2 %parent_factor.1 = f32[1,4608,256]{2,1,0:T(8,128)S(1)} custom-call(f32[1,256,256]{2,1,0:T(8,128)S(1)} %copy.92.a_ref, f32[1,4608,256]{2,1,0:T(8,128)} %maximum_bitcast_fusion.x_ref), custom_call_target="tpu_custom_call" | custom-call | tf_op jit(solution)/shard_map/parent_factor/pallas_call | solution.py:97
  2218.0 10.8 fusion.8
  2228.8 76.2 %subtract_select_fusion = f32[3072,1536]{0,1:T(8,128)} fusion(f32[3072,1536]{0,1:T(8,128)} %fusion.8, f32[3072,1536]{0,1:T(8,128)} %fusion, f32[1536,1024]{1,0:T(8,128)} %get-tuple-element.85, f32[1536,1024]{1,0:T(8,128)} %get-tuple-element.84, f32[1536,1024]{1,0:T(8,128)} %get-tuple-element.83, f32[1536,1024]{1,0:T(8,128)S(1)} %bitcast.214, ...), kind=kOutput, calls=%fused_computation.19 | convolution fusion | flops 58019807232 | bytes 94376448 | tf_op jit(solution)/shard_map/merged/dot_general | solution.py:18
  2305.0 18.8 copy.96
  2325.5 2.6 copy.93
  (154 shorter events, 23.8 us)
Async XLA Ops:
  8.0 24.3 %sort.37.cloned.1.call-start = ((), (), s32[]{:S(2)}) async-start(), calls=%async_computation.9 | async-start | bytes 393248 | tf_op jit(solution)/shard_map/orders/jit(argsort)/sort | solution.py:135
  10.9 195.2 %all-reduce.7.cloned.1.call-start = ((), (), s32[]{:S(2)}) async-start(), calls=%async_computation.3 | async-start | bytes 16777216 | tf_op jit(solution)/shard_map/corner/psum | solution.py:155
  23.5 680.1 %all-gather.3.cloned.1.call-start = ((), (), s32[]{:S(2)}) async-start(), calls=%async_computation.8 | async-start | bytes 18874368 | tf_op jit(solution)/shard_map/factor_rows/all_gather | solution.py:191
  79.3 9.8 collective-permute-start
  81.7 29.9 %collective-permute-start.1 = (f32[2,256,1024]{2,1,0:T(8,128)}, f32[2,256,1024]{2,1,0:T(8,128)}, u32[]{:S(2)}, u32[]{:S(2)}) collective-permute-start(f32[2,256,1024]{2,1,0:T(8,128)} %get-tuple-element.87), channel_id=1, source_target_pairs={{0,16},{1,17},{2,18},{3,19},{4,20},{5,21},{6,22},{7,23}} | collective-permute-start | bytes 6291464 | tf_op jit(solution)/shard_map/own_rows/ppermute | solution.py:164
  86.4 50.5 %collective-permute-start.2 = (f32[2,256,1024]{2,1,0:T(8,128)}, f32[2,256,1024]{2,1,0:T(8,128)}, u32[]{:S(2)}, u32[]{:S(2)}) collective-permute-start(f32[2,256,1024]{2,1,0:T(8,128)} %get-tuple-element.88), channel_id=1, source_target_pairs={{0,24},{1,25},{2,26},{3,27},{4,28},{5,29},{6,30},{7,31}} | collective-permute-start | bytes 6291464 | tf_op jit(solution)/shard_map/own_rows/ppermute | solution.py:164
  89.1 22.6 copy-start.8
  362.2 1.6 copy-start.9
  363.8 0.6 copy-start.17
  552.3 5.9 copy-start.10
  552.3 399.9 %all-to-all-start.2 = ((f32[32,2,128,512]{3,2,1,0:T(8,128)}), f32[32,2,128,512]{3,2,1,0:T(8,128)}, u32[]{:S(2)}, u32[]{:S(2)}) async-start(f32[32,2,128,512]{3,2,1,0:T(8,128)} %bitcast.204), calls=%async_computation.2 | async-start | bytes 33554432 | tf_op jit(solution)/shard_map/exchange/all_to_all | solution.py:177
  558.1 1160.8 %all-reduce.9.cloned.1.call-start = ((), (), s32[]{:S(2)}) async-start(), calls=%async_computation.4 | async-start | bytes 16777216 | tf_op jit(solution)/shard_map/factor_rows/psum | solution.py:195
  730.3 0.7 copy-start.20
  730.3 0.7 copy-start.19
  730.3 26.0 %copy-start.6 = (f32[2,256,1024]{2,1,0:T(8,128)S(1)}, f32[2,256,1024]{2,1,0:T(8,128)}, u32[]{:S(2)}) copy-start(f32[2,256,1024]{2,1,0:T(8,128)} %compare_select_fusion) | copy-start | bytes 6291460
  730.3 1134.1 %sort.39.cloned.1.call-start = ((), (), s32[]{:S(2)}) async-start(), calls=%async_computation.10 | async-start | bytes 98336 | tf_op jit(solution)/shard_map/outputs/jit(argsort)/sort | solution.py:255
  738.4 289.2 %copy-start.1 = (s32[3072]{0:T(1024)}, s32[3072]{0:T(1024)S(1)}, u32[]{:S(2)}) copy-start(s32[3072]{0:T(1024)S(1)} %reshape.542) | copy-start | bytes 36868
  738.4 423.6 %copy-start.11 = (pred[2,1536]{1,0:T(4,128)(4,1)}, pred[2,1536]{1,0:T(4,128)(4,1)S(1)}, u32[]{:S(2)}) copy-start(pred[2,1536]{1,0:T(4,128)(4,1)S(1)} %reshape.452) | copy-start | bytes 9220
  745.7 7.4 copy-start.13
  952.2 905.4 %all-to-all-start = ((f32[1,2,256,8,128]{4,2,1,0,3:T(8,128)}), f32[1,2,256,8,128]{4,2,1,0,3:T(8,128)}, u32[]{:S(2)}, u32[]{:S(2)}) async-start(f32[1,2,256,8,128]{4,2,1,0,3:T(8,128)} %copy.76), calls=%async_computation | async-start | bytes 4194304 | tf_op jit(solution)/shard_map/outputs/all_to_all | solution.py:251
  963.3 1024.3 %all-reduce.11.cloned.1.call-start = ((), (), s32[]{:S(2)}) async-start(), calls=%async_computation.5 | async-start | bytes 6291456 | tf_op jit(solution)/shard_map/parent_strips/psum | solution.py:228
  1382.8 36.8 %copy-start.15 = (pred[2,3072]{1,0:T(4,128)(4,1)S(1)}, pred[2,3072]{1,0:T(4,128)(4,1)}, u32[]{:S(2)}) copy-start(pred[2,3072]{1,0:T(4,128)(4,1)} %broadcast_compare_fusion) | copy-start | bytes 18436
  1449.0 25.9 %copy-start.5 = (f32[8,2,1,128,1024]{4,3,2,1,0:T(8,128)S(1)}, f32[8,2,1,128,1024]{4,3,2,1,0:T(8,128)}, u32[]{:S(2)}) copy-start(f32[8,2,1,128,1024]{4,3,2,1,0:T(8,128)} %get-tuple-element.77) | copy-start | bytes 25165828
  1474.9 4.1 copy-start.4
  1479.0 93.6 %copy-start.16 = (pred[2,1536]{1,0:T(4,128)(4,1)S(1)}, pred[2,1536]{1,0:T(4,128)(4,1)}, u32[]{:S(2)}) copy-start(pred[2,1536]{1,0:T(4,128)(4,1)} %broadcast_compare_fusion.3) | copy-start | bytes 9220
  1594.7 8.3 copy-start.3
  1603.0 93.9 %copy-start.14 = (pred[2,1536]{1,0:T(4,128)(4,1)S(1)}, pred[2,1536]{1,0:T(4,128)(4,1)}, u32[]{:S(2)}) copy-start(pred[2,1536]{1,0:T(4,128)(4,1)} %copy-done.13) | copy-start | bytes 9220
  1707.1 11.9 copy-start.2
  1718.9 94.2 %copy-start.12 = (pred[2,1536]{1,0:T(4,128)(4,1)S(1)}, pred[2,1536]{1,0:T(4,128)(4,1)}, u32[]{:S(2)}) copy-start(pred[2,1536]{1,0:T(4,128)(4,1)} %copy-done.11) | copy-start | bytes 9220
  1857.6 6.9 copy-start.18
  1860.7 29.3 %all-to-all-start.1 = ((f32[4,2,2,256,128]{4,3,1,2,0:T(8,128)}), f32[4,2,2,256,128]{4,3,1,2,0:T(8,128)S(1)}, u32[]{:S(2)}, u32[]{:S(2)}) async-start(f32[4,2,2,256,128]{4,3,1,2,0:T(8,128)} %copy.77), calls=%async_computation.1 | async-start | bytes 4194304 | tf_op jit(solution)/shard_map/outputs/all_to_all | solution.py:253
  1864.4 167.4 %all-reduce.15.cloned.1.call-start = ((), (), s32[]{:S(2)}) async-start(), calls=%async_computation.7 | async-start | bytes 3145728 | tf_op jit(solution)/shard_map/parent_strips/psum | solution.py:227
  1890.0 1.3 copy-start.7
  1948.0 215.7 %all-reduce.13.cloned.1.call-start = ((), (), s32[]{:S(2)}) async-start(), calls=%async_computation.6 | async-start | bytes 524288 | tf_op jit(solution)/shard_map/parent_strips/psum | solution.py:229
  2164.7 64.1 %slice-start.1 = ((s8[6291456]{0:T(1024)(128)(4,1)}), s8[2097152]{0:T(1024)(128)(4,1)S(1)}, s32[]{:S(2)}) async-start(s8[6291456]{0:T(1024)(128)(4,1)} %bitcast.213), calls=%async_computation.14 | async-start | bytes 4194304
  2218.0 10.8 copy-start
  2218.0 10.8 slice-start.2
  2305.0 18.8 slice-start
Sparse Core Ops, SparseCore 0:
  11.9 7.1 sort.41.cloned.1.call-done
  363.9 277.7 all-gather.2
  755.2 7.4 sort.43.cloned.1.call-done
  1857.7 129.8 all-reduce.10
  1990.0 41.7 all-reduce.14
  2038.6 124.9 all-reduce.12
  (2 shorter events, 0.0 us)
Sparse Core Ops, SparseCore 1:
  23.6 182.5 all-reduce.6
  730.4 229.5 all-reduce.8
